TPU v7x, 32 devices: a whole 2x2x4 slice. The times are simulated.
32 devices in a mesh: groups: 2 (over x), dev: 16 (over z, y, core).
Axes of the slice: x: 2, y: 2, z: 4, core: 2. Of those that a mesh axis runs over, the one named last changes fastest.
Arguments:
- tokens: bfloat16 [64, 8192], P(('groups', 'dev')), parts along dimension 0, may hold values from -6 to 6
- gate_weight: bfloat16 [8192, 14336], P(None, 'dev'), may hold values from -0.0625 to 0.0625
- up_weight: bfloat16 [8192, 14336], P(None, 'dev'), may hold values from -0.0625 to 0.0625
- down_weight: bfloat16 [14336, 8192], P('dev'), may hold values from -0.0625 to 0.0625
- grad_in: bfloat16 [32, 14336, 32], P(('groups', 'dev')), parts along dimension 0, may hold values from -6 to 6
- grad_out: bfloat16 [32, 32, 8192], P(('groups', 'dev')), parts along dimension 0, may hold values from -6 to 6
- adapter_in: float32 [16, 14336, 32], P('groups', 'dev'), parts along dimension 0, may hold values from -6 to 6
- adapter_out: float32 [16, 32, 8192], P('groups', None, 'dev'), parts along dimension 0, may hold values from -6 to 6
- moment_in: float32 [16, 14336, 32], P('groups', 'dev'), parts along dimension 0, may hold values from -3 to 3
- moment_out: float32 [16, 32, 8192], P('groups', None, 'dev'), parts along dimension 0, may hold values from -3 to 3
- second_in: float32 [16, 14336, 32], P('groups', 'dev'), parts along dimension 0, may hold values from 0.001 to 0.1
- second_out: float32 [16, 32, 8192], P('groups', None, 'dev'), parts along dimension 0, may hold values from 0.001 to 0.1
- tenants: int32 [32], P('groups'), parts along dimension 0, may hold values from 0 to 7, never falling along the last dimension, each value on 1 to 8 neighbouring positions
- placement: int32 [32, 4], P('groups'), parts along dimension 0, may hold values from 0 to 7
- row_slot: int32 [64], P(('groups', 'dev')), parts along dimension 0, may hold values from 0 to 3
Outputs:
- layer_out: bfloat16 [64, 8192], P(('groups', 'dev')), parts along dimension 0
- new_in: float32 [16, 14336, 32], P('groups', 'dev'), parts along dimension 0
- new_out: float32 [16, 32, 8192], P('groups', None, 'dev'), parts along dimension 0
There are 2 independent parts, one for each index of `groups`. A program takes and returns all parts, laid end to end along the dimension named above; an argument that names none is the same for every part. Nothing has to cross between parts.
Inputs may be any that keep to these rules, and one draw needn't show every extreme that they name: tenants never fall from one training device to the next; every adapter has 1 to 8 training devices, and one has exactly 8.
All inputs are finite; a program needn't handle non-finite values.
Results may differ from a plain program's by a relative error of at most 0.0062.
Values may be sent and summed in bfloat16 or wider, within the bound.
A program may use at most 192 MiB of HBM per device.

v0:
```python
import math

import jax
import jax.numpy as jnp
from jax import lax
from jax.sharding import PartitionSpec as P

FFW = 14336


first_decay = 0.9
second_decay = 0.999
learn_rate = 0.2
adam_eps = 1e-08
first_fix = 1.0 - 0.9**10
second_fix = 1.0 - 0.999**10


def adam_update(current, moment, second, gradient):
    moment_new = first_decay * moment + (1.0 - first_decay) * gradient
    second_new = second_decay * second + (1.0 - second_decay) * gradient * gradient
    return current - learn_rate * (moment_new / first_fix) / (
        jnp.sqrt(second_new / second_fix) + adam_eps
    )


def shards(
    tokens,
    gate_weight,
    up_weight,
    down_weight,
    grad_in,
    grad_out,
    adapter_in,
    adapter_out,
    moment_in,
    moment_out,
    second_in,
    second_out,
    tenants,
    placement,
    row_slot,
):
    workers = lax.axis_size("dev")
    device_index = lax.axis_index("dev")
    adapter_count = adapter_in.shape[0]
    hidden_block = adapter_in.shape[1]
    adapter_rank = adapter_in.shape[2]
    column_block = adapter_out.shape[2]
    slot_count = placement.shape[1]
    inv_rank = 1.0 / math.sqrt(adapter_rank)
    flat_in = grad_in.reshape(1, workers, hidden_block * adapter_rank)
    flat_out = grad_out.reshape(adapter_rank, workers, column_block)
    got_in, got_out = (
        lax.all_to_all(flat_in, "dev", split_axis=1, concat_axis=1, tiled=True),
        lax.all_to_all(flat_out, "dev", split_axis=1, concat_axis=1, tiled=True),
    )
    owners = (tenants[None, :] == jnp.arange(adapter_count, dtype=jnp.int32)[:, None]).astype(
        jnp.bfloat16
    )
    summed_in = jnp.einsum(
        "an,nk->ak", owners, got_in[0], preferred_element_type=jnp.float32
    ).reshape(adapter_count, hidden_block, adapter_rank)
    summed_out = jnp.einsum("an,knc->akc", owners, got_out, preferred_element_type=jnp.float32)
    new_in = adam_update(adapter_in, moment_in, second_in, summed_in)
    new_out = adam_update(adapter_out, moment_out, second_out, summed_out)
    serve_in = new_in.astype(jnp.bfloat16)
    serve_out = new_out.astype(jnp.bfloat16)
    chosen_own = placement[device_index][row_slot]
    hot_own = (chosen_own[:, None] == jnp.arange(adapter_count, dtype=jnp.int32)[None, :]).astype(
        jnp.bfloat16
    )
    all_tokens, hot_all = (
        lax.all_gather(tokens, "dev", axis=0, tiled=True),
        lax.all_gather(hot_own, "dev", axis=0, tiled=True),
    )
    gate = jnp.dot(all_tokens, gate_weight, preferred_element_type=jnp.float32)
    upward = jnp.dot(all_tokens, up_weight, preferred_element_type=jnp.float32)
    hidden = (jax.nn.silu(gate) * upward).astype(jnp.bfloat16)
    every = jnp.einsum("rf,afk->rak", hidden, serve_in, preferred_element_type=jnp.float32)
    inner_part = jnp.sum(every * hot_all.astype(jnp.float32)[:, :, None], axis=1) * (
        1.0 / math.sqrt(FFW)
    )
    lifted = lax.psum_scatter(inner_part, "dev", scatter_dimension=0, tiled=True).astype(
        jnp.bfloat16
    )
    partial_sum = jnp.dot(hidden, down_weight, preferred_element_type=jnp.float32)
    summed_rows = lax.psum_scatter(partial_sum, "dev", scatter_dimension=0, tiled=True)
    outgoing = serve_out[placement]
    arrived = lax.all_to_all(outgoing, "dev", split_axis=0, concat_axis=3, tiled=True)
    slot_pick = (row_slot[:, None] == jnp.arange(slot_count, dtype=jnp.int32)[None, :]).astype(
        jnp.float32
    )
    delta_every = jnp.einsum("rk,skd->rsd", lifted, arrived[0], preferred_element_type=jnp.float32)
    delta = jnp.sum(delta_every * slot_pick[:, :, None], axis=1)
    layer_out = (summed_rows + delta * inv_rank).astype(jnp.bfloat16)
    return (layer_out, new_in, new_out)


def solution(mesh):
    in_specs = (
        P(("groups", "dev"), None),
        P(None, "dev"),
        P(None, "dev"),
        P("dev", None),
        P(("groups", "dev"), None, None),
        P(("groups", "dev"), None, None),
        P("groups", "dev", None),
        P("groups", None, "dev"),
        P("groups", "dev", None),
        P("groups", None, "dev"),
        P("groups", "dev", None),
        P("groups", None, "dev"),
        P("groups"),
        P("groups", None),
        P(("groups", "dev")),
    )
    out_specs = (P(("groups", "dev"), None), P("groups", "dev", None), P("groups", None, "dev"))
    return jax.shard_map(shards, mesh=mesh, in_specs=in_specs, out_specs=out_specs, check_vma=False)
```

profile of v0, /device:TPU:0, one launch (start us, length us, event | category | flops | bytes accessed | tf_op | source)
XLA Modules:
  0.0 250.5 jit_solution(16425304051369774582)
XLA Ops:
  7.2 1.3 copy.77
  8.5 1.1 copy.67
  9.5 7.4 %all-to-all-start.1 = ((bf16[32,16,512]{2,0,1:T(8,128)(2,1)}), bf16[32,16,512]{2,0,1:T(8,128)(2,1)S(1)}, u32[]{:S(2)}, u32[]{:S(2)}) async-start(bf16[32,16,512]{2,0,1:T(8,128)(2,1)} %copy.67), calls=%async_computation.1 | async-start | bytes 1048576 | tf_op jit(solution)/shard_map/all_to_all | solution.py:56
  16.9 3.0 %copy.59 = bf16[1,14336,32]{2,1,0:T(8,128)(2,1)} copy(bf16[1,14336,32]{1,2,0:T(8,128)(2,1)S(1)} %copy-done.1) | data formatting | bytes 1835008 | tf_op args[4]
  20.0 5.8 %reshape.69 = bf16[1,16,28672]{2,0,1:T(2,128)(2,1)S(1)} reshape(bf16[1,14336,32]{2,1,0:T(8,128)(2,1)} %copy.59) | data formatting | bytes 1835008 | tf_op jit(solution)/shard_map/reshape | solution.py:52
  25.8 0.5 broadcast.44
  26.3 6.2 %reduce.2 = bf16[16,28672]{1,0:T(8,128)(2,1)S(1)} reduce(bf16[16,1,28672]{2,1,0:T(2,128)(2,1)S(1)} %bitcast.50, bf16[]{:T(256)} %broadcast.44), dimensions={1}, to_apply=%bitcast.31.reduce_sub_computation | reduce | bytes 1835010
  32.6 1.6 reshape.73
  34.2 6.0 %all-to-all-start = ((bf16[16,2,14336]{2,1,0:T(2,128)(2,1)}), bf16[16,2,14336]{2,1,0:T(2,128)(2,1)S(1)}, u32[]{:S(2)}, u32[]{:S(2)}) async-start(bf16[16,2,14336]{2,1,0:T(2,128)(2,1)} %reshape.73), calls=%async_computation | async-start | bytes 1835008 | tf_op jit(solution)/shard_map/all_to_all | solution.py:55
  40.2 33.3 %all-gather = bf16[16,2,8192]{2,1,0:T(2,128)(2,1)S(1)} all-gather(bf16[1,2,8192]{2,1,0:T(2,128)(2,1)S(1)} %bitcast.54), channel_id=1, replica_groups=mesh['groups'=2,'dev'=16] {'dev'}, dimensions={0}, use_global_device_ids=true | all-gather | bytes 557056 | tf_op jit(solution)/shard_map/all_gather | solution.py:74
  73.9 2.9 %fusion.35 = (bf16[8,32,512]{2,0,1:T(8,128)(2,1)S(1)}, f32[8,32,512]{2,0,1:T(8,128)S(1)}) fusion(f32[8,32,512]{2,1,0:T(8,128)} %param.26, bf16[32,16,512]{2,0,1:T(8,128)(2,1)} %copy-done.2, s32[16]{0:T(128)S(1)} %copy-done.6, f32[8,32,512]{2,1,0:T(8,128)} %param.24, f32[8,32,512]{2,1,0:T(8,128)} %param.22), kind=kOutput, calls=%fused_computation.53 | convolution fusion | flops 5898368 | bytes 2883648 | tf_op jit(solution)/shard_map/an,knc->akc/dot_general | solution.py:64
  76.8 2.0 gather_fusion.1
  78.9 0.9 copy-done
  79.8 5.4 %all-to-all-start.2 = ((bf16[16,4,32,512]{3,2,1,0:T(8,128)(2,1)}), bf16[16,4,32,512]{3,2,1,0:T(8,128)(2,1)S(1)}, u32[]{:S(2)}, u32[]{:S(2)}) async-start(bf16[16,4,32,512]{3,2,1,0:T(8,128)(2,1)} %bitcast.7), calls=%async_computation.2 | async-start | bytes 4194304 | tf_op jit(solution)/shard_map/all_to_all | solution.py:90
  85.4 7.7 %fusion.37 = f32[32,896]{1,0:T(8,128)S(1)} fusion(bf16[32,8192]{1,0:T(8,128)(2,1)S(1)} %reshape.62, bf16[8192,896]{1,0:T(8,128)(2,1)} %param.16), kind=kOutput, calls=%fused_computation.55 | convolution fusion | flops 469762048 | bytes 15319040 | tf_op jit(solution)/shard_map/dot_general | solution.py:77
  93.1 7.7 %fusion.1 = bf16[32,896]{1,0:T(8,128)(2,1)S(1)} fusion(bf16[32,8192]{1,0:T(8,128)(2,1)S(1)} %reshape.62, bf16[8192,896]{1,0:T(8,128)(2,1)} %param.17, f32[32,896]{1,0:T(8,128)S(1)} %fusion.37), kind=kOutput, calls=%fused_computation.7 | convolution fusion | flops 469934080 | bytes 15376384 | tf_op jit(solution)/shard_map/dot_general | solution.py:78
  100.8 3.7 %fusion.38 = f32[32,8192]{1,0:T(8,128)} fusion(bf16[32,896]{1,0:T(8,128)(2,1)S(1)} %fusion.1, bf16[896,8192]{1,0:T(8,128)(2,1)S(1)} %bitcast.47), kind=kOutput, calls=%fused_computation.56 | convolution fusion | flops 469762048 | bytes 15785984 | tf_op jit(solution)/shard_map/dot_general | solution.py:87
  104.7 0.6 gather_fusion
  105.4 32.2 %all-gather.1 = bf16[16,2,8]{2,1,0:T(2,128)(2,1)S(1)} all-gather(bf16[1,2,8]{2,1,0:T(2,128)(2,1)S(1)} %fusion.34), channel_id=1, replica_groups=mesh['groups'=2,'dev'=16] {'dev'}, dimensions={0}, use_global_device_ids=true | all-gather | bytes 544 | tf_op jit(solution)/shard_map/all_gather | solution.py:75
  137.7 0.6 dynamic-slice
  138.9 1.1 copy.75
  140.0 5.6 %reshape.74 = bf16[16,1,28672]{2,1,0:T(2,128)(2,1)} reshape(bf16[16,2,14336]{2,1,0:T(2,128)(2,1)} %copy-done) | data formatting | bytes 1835008
  145.7 3.4 %copy.109 = bf16[1,16,28672]{2,1,0:T(8,128)(2,1)} copy(bf16[1,16,28672]{2,0,1:T(2,128)(2,1)} %bitcast.49) | data formatting | bytes 1835008
  149.1 4.9 %dot_general.29 = bf16[896,32,16]{1,0,2:T(8,128)(2,1)} reshape(bf16[28672,16]{0,1:T(8,128)(2,1)} %bitcast.51) | data formatting | bytes 1835008 | tf_op jit(solution)/shard_map/an,nk->ak/dot_general | solution.py:61
  154.0 4.7 %copy.61 = bf16[896,32,16]{0,2,1:T(8,128)(2,1)} copy(bf16[896,32,16]{1,0,2:T(8,128)(2,1)} %dot_general.29) | data formatting | bytes 1835008 | tf_op jit(solution)/shard_map/an,nk->ak/dot_general | solution.py:61
  158.8 4.2 %fusion.36 = (bf16[8,896,32]{1,0,2:T(8,128)(2,1)S(1)}, f32[8,896,32]{1,0,2:T(8,128)S(1)}) fusion(f32[8,896,32]{1,2,0:T(8,128)} %param.25, bf16[896,32,16]{0,2,1:T(8,128)(2,1)} %copy.61, s32[16]{0:T(128)S(1)} %copy-done.6, f32[8,896,32]{1,2,0:T(8,128)} %param.23, f32[8,896,32]{1,2,0:T(8,128)} %param.21), kind=kOutput, calls=%fused_computation.54 | convolution fusion | flops 10322048 | bytes 5046336 | tf_op jit(solution)/shard_map/an,nk->ak/dot_general | solution.py:61
  162.9 1.1 copy.74
  164.0 0.5 fusion.2
  164.6 71.6 %all-reduce.1 = bf16[32,32]{1,0:T(8,128)(2,1)S(1)} all-reduce(f32[32,32]{1,0:T(8,128)S(1)} %broadcast_multiply_fusion), channel_id=3, replica_groups=mesh['groups'=2,'dev'=16] {'dev'}, use_global_device_ids=true, to_apply=%region_2.3.clone | all-reduce | flops 1024 | bytes 6144
  236.2 2.5 %copy.73 = bf16[1,4,32,16,512]{4,3,2,1,0:T(8,128)(2,1)} copy(bf16[1,4,32,16,512]{4,2,1,3,0:T(8,128)(2,1)S(1)} %bitcast.48) | data formatting | bytes 4194304 | tf_op jit(solution)/shard_map/all_to_all | solution.py:90
  238.7 2.9 %squeeze.11 = bf16[4,32,8192]{2,1,0:T(8,128)(2,1)S(1)} reshape(bf16[1,4,32,16,512]{4,3,2,1,0:T(8,128)(2,1)} %copy.73) | data formatting | bytes 4194304 | tf_op jit(solution)/shard_map/squeeze | solution.py:94
  242.0 1.6 fusion.24
  (44 shorter events, 1.6 us)
Async XLA Ops:
  7.2 9.8 %copy-start.1 = (bf16[1,14336,32]{1,2,0:T(8,128)(2,1)S(1)}, bf16[1,14336,32]{1,2,0:T(8,128)(2,1)}, u32[]{:S(2)}) copy-start(bf16[1,14336,32]{1,2,0:T(8,128)(2,1)} %param.19) | copy-start | bytes 2752516
  9.5 24.6 %all-to-all-start.1 = ((bf16[32,16,512]{2,0,1:T(8,128)(2,1)}), bf16[32,16,512]{2,0,1:T(8,128)(2,1)S(1)}, u32[]{:S(2)}, u32[]{:S(2)}) async-start(bf16[32,16,512]{2,0,1:T(8,128)(2,1)} %copy.67), calls=%async_computation.1 | async-start | bytes 1048576 | tf_op jit(solution)/shard_map/all_to_all | solution.py:56
  25.8 14.4 %copy-start.3 = (bf16[2,8192]{1,0:T(2,128)(2,1)S(1)}, bf16[2,8192]{1,0:T(2,128)(2,1)}, u32[]{:S(2)}) copy-start(bf16[2,8192]{1,0:T(2,128)(2,1)} %param.15) | copy-start | bytes 98308
  26.3 47.4 %copy-start.4 = (s32[16,4]{0,1:T(4,128)S(1)}, s32[16,4]{0,1:T(4,128)}, u32[]{:S(2)}) copy-start(s32[16,4]{0,1:T(4,128)} %param.28) | copy-start | bytes 772
  26.3 47.6 %copy-start.6 = (s32[16]{0:T(128)S(1)}, s32[16]{0:T(128)}, u32[]{:S(2)}) copy-start(s32[16]{0:T(128)} %param.27) | copy-start | bytes 196
  34.2 39.7 %copy-start.2 = (bf16[32,16,512]{2,0,1:T(8,128)(2,1)}, bf16[32,16,512]{2,0,1:T(8,128)(2,1)S(1)}, u32[]{:S(2)}) copy-start(bf16[32,16,512]{2,0,1:T(8,128)(2,1)S(1)} %all-to-all-done.1) | copy-start | bytes 1572868
  34.2 44.7 %all-to-all-start = ((bf16[16,2,14336]{2,1,0:T(2,128)(2,1)}), bf16[16,2,14336]{2,1,0:T(2,128)(2,1)S(1)}, u32[]{:S(2)}, u32[]{:S(2)}) async-start(bf16[16,2,14336]{2,1,0:T(2,128)(2,1)} %reshape.73), calls=%async_computation | async-start | bytes 1835008 | tf_op jit(solution)/shard_map/all_to_all | solution.py:55
  78.8 0.9 copy-start
  79.8 156.4 %all-to-all-start.2 = ((bf16[16,4,32,512]{3,2,1,0:T(8,128)(2,1)}), bf16[16,4,32,512]{3,2,1,0:T(8,128)(2,1)S(1)}, u32[]{:S(2)}, u32[]{:S(2)}) async-start(bf16[16,4,32,512]{3,2,1,0:T(8,128)(2,1)} %bitcast.7), calls=%async_computation.2 | async-start | bytes 4194304 | tf_op jit(solution)/shard_map/all_to_all | solution.py:90
  85.1 156.9 %all-reduce.4.cloned.1.call-start = ((), (), s32[]{:S(2)}) async-start(), calls=%async_computation.3 | async-start | bytes 2097152
  85.4 15.4 %slice-start = ((s8[14680064]{0:T(1024)(128)(4,1)}), s8[4194304]{0:T(1024)(128)(4,1)S(1)}, s32[]{:S(2)}) async-start(s8[14680064]{0:T(1024)(128)(4,1)} %bitcast.46), calls=%async_computation.4 | async-start | bytes 8388608
  85.4 15.4 %slice-start.1 = ((s8[14680064]{0:T(1024)(128)(4,1)}), s8[4194304]{0:T(1024)(128)(4,1)S(1)}, s32[]{:S(2)}) async-start(s8[14680064]{0:T(1024)(128)(4,1)} %bitcast.46), calls=%async_computation.5 | async-start | bytes 8388608
  85.4 15.4 %slice-start.2 = ((s8[14680064]{0:T(1024)(128)(4,1)}), s8[4194304]{0:T(1024)(128)(4,1)S(1)}, s32[]{:S(2)}) async-start(s8[14680064]{0:T(1024)(128)(4,1)} %bitcast.46), calls=%async_computation.6 | async-start | bytes 8388608
  93.1 7.7 %slice-start.3 = ((s8[14680064]{0:T(1024)(128)(4,1)}), s8[2097152]{0:T(1024)(128)(4,1)S(1)}, s32[]{:S(2)}) async-start(s8[14680064]{0:T(1024)(128)(4,1)} %bitcast.46), calls=%async_computation.7 | async-start | bytes 4194304
  100.8 3.9 %copy-start.5 = (s32[2]{0:T(128)S(1)}, s32[2]{0:T(128)}, u32[]{:S(2)}) copy-start(s32[2]{0:T(128)} %param.29) | copy-start | bytes 28
  100.8 36.9 %copy-start.7 = (u32[32]{0:T(128)S(1)}, u32[32]{0:T(128)}, u32[]{:S(2)}) copy-start(u32[32]{0:T(128)} %constant.58) | copy-start | bytes 388
Sparse Core Ops, SparseCore 0:
  104.6 103.4 all-reduce.3
where the time goes:
time: 251 us; the launch traced here: 250 us
  blocking collectives  137 us (55%)
  local copies, waits for them, and re-layouts  44.5 us (18%)
  matrix products  26.9 us (11%)
  starting transfers between devices  19 us (8%)
  between operations  15 us (6%)
  other arithmetic  7.96 us (3%)
    unnamed x1, blocking collectives  71.6 us
    all_gather x1, blocking collectives, shards(): lax.all_gather(tokens, 'dev', axis=0, tiled=True)  33.3 us
    all_gather x1, blocking collectives, shards(): lax.all_gather(hot_own, 'dev', axis=0, tiled=True)  32.2 us
    unnamed x34, local copies, waits for them, and re-layouts  19.5 us
    dot_general x2, local copies, waits for them, and re-layouts, shards(): jnp.einsum('an,nk->ak', owners, got_in[0], preferred_element_type=jnp.flo...  9.67 us
    dot_general x1, matrix products, shards(): upward = jnp.dot(all_tokens, up_weight, preferred_element_type=jnp.float32)  7.66 us
    dot_general x1, matrix products, shards(): gate = jnp.dot(all_tokens, gate_weight, preferred_element_type=jnp.float32)  7.65 us
    all_to_all x1, starting transfers between devices, shards(): lax.all_to_all(flat_out, 'dev', split_axis=1, concat_axis=1, tiled=True)  7.39 us
  transfers between devices with their start and end apart: 4, of which 0 were waited for; matrix products, arithmetic and copies ran while one was open for 30% of the time, Pallas kernels for 0%

commit v1 on v0

--- a/solution.py
+++ b/solution.py
@@ -1,8 +1,11 @@
+import functools
 import math
 
 import jax
 import jax.numpy as jnp
 from jax import lax
+from jax.experimental import pallas as pl
+from jax.experimental.pallas import tpu as pltpu
 from jax.sharding import PartitionSpec as P
 
 FFW = 14336
@@ -97,6 +100,446 @@
     return (layer_out, new_in, new_out)
 
 
+MESH = pl.DeviceIdType.MESH
+CHUNKS = 8
+
+
+def fused_kernel(
+    n,
+    payload,
+    gate,
+    up,
+    down,
+    grad_in,
+    grad_out,
+    adapter_in,
+    moment_in,
+    second_in,
+    adapter_out,
+    moment_out,
+    second_out,
+    owners,
+    layer,
+    new_in,
+    new_out,
+    gate_s,
+    up_s,
+    down_s,
+    tok_s,
+    gin_s,
+    gout_s,
+    ad_in,
+    ad_out,
+    new_in_s,
+    new_out_s,
+    serve_in,
+    serve_out,
+    accg,
+    accu,
+    part,
+    own,
+    got_part,
+    got_inner,
+    rows_out,
+    got_rows,
+    weight_sem,
+    local_sem,
+    tok_send,
+    tok_recv,
+    gin_send,
+    gin_recv,
+    gout_send,
+    gout_recv,
+    part_send,
+    part_recv,
+    inner_send,
+    inner_recv,
+    rows_send,
+    rows_recv,
+):
+    me = lax.axis_index("dev")
+    adapters, rank, hidden_block = ad_in.shape[1:]
+    column_block = ad_out.shape[3]
+    lanes = adapters * rank
+    width = payload.shape[1] - 128
+    depth = gate_s.shape[1]
+    row_count = accg.shape[0]
+
+    def other(s):
+        return lax.rem(me + s, n)
+
+    def remote(src, dst, send, recv, peer):
+        return pltpu.make_async_remote_copy(
+            src_ref=src,
+            dst_ref=dst,
+            send_sem=send,
+            recv_sem=recv,
+            device_id={"dev": peer},
+            device_id_type=MESH,
+        )
+
+    def each(body):
+        def step(s, carry):
+            body(other(s))
+            return carry
+
+        lax.fori_loop(1, n, step, 0)
+
+    def hid(j):
+        return pl.ds(pl.multiple_of(j * hidden_block, 128), hidden_block)
+
+    def col(j):
+        return pl.ds(pl.multiple_of(j * column_block, 128), column_block)
+
+    def send_tok(p):
+        return remote(payload, tok_s.at[me], tok_send.at[p], tok_recv.at[me], p)
+
+    def send_gin(p):
+        return remote(
+            grad_in.at[:, hid(p)], gin_s.at[me], gin_send.at[p], gin_recv.at[me], p
+        )
+
+    def send_gout(p):
+        return remote(
+            grad_out.at[:, col(p)], gout_s.at[me], gout_send.at[p], gout_recv.at[me], p
+        )
+
+    def send_part(p):
+        return remote(part.at[p], got_part.at[me], part_send.at[p], part_recv.at[me], p)
+
+    def send_inner(p):
+        return remote(
+            got_inner.at[me], got_inner.at[me], inner_send.at[p], inner_recv.at[me], p
+        )
+
+    def send_rows(p):
+        return remote(rows_out.at[p], got_rows.at[me], rows_send.at[p], rows_recv.at[me], p)
+
+    def arrived(buf, send, recv):
+        each(lambda p: remote(buf.at[p], buf.at[p], send.at[p], recv.at[p], p).wait_recv())
+
+    def gate_copy(c):
+        rows = pl.ds(pl.multiple_of(c * depth, 128), depth)
+        return pltpu.make_async_copy(gate.at[rows, :], gate_s.at[c], weight_sem.at[c])
+
+    def up_copy(c):
+        rows = pl.ds(pl.multiple_of(c * depth, 128), depth)
+        return pltpu.make_async_copy(up.at[rows, :], up_s.at[c], weight_sem.at[CHUNKS + c])
+
+    def down_copy(s):
+        return pltpu.make_async_copy(
+            down.at[:, col(other(s))], down_s.at[s], weight_sem.at[2 * CHUNKS + s]
+        )
+
+    own_tok = pltpu.make_async_copy(payload, tok_s.at[me], local_sem.at[0])
+    own_gin = pltpu.make_async_copy(grad_in.at[:, hid(me)], gin_s.at[me], local_sem.at[1])
+    own_gout = pltpu.make_async_copy(grad_out.at[:, col(me)], gout_s.at[me], local_sem.at[2])
+    loads = [
+        pltpu.make_async_copy(ref, dst, local_sem.at[3 + i])
+        for i, (ref, dst) in enumerate(
+            [
+                (adapter_in, ad_in.at[0]),
+                (moment_in, ad_in.at[1]),
+                (second_in, ad_in.at[2]),
+                (adapter_out, ad_out.at[0]),
+                (moment_out, ad_out.at[1]),
+                (second_out, ad_out.at[2]),
+            ]
+        )
+    ]
+    store_in = pltpu.make_async_copy(new_in_s, new_in, local_sem.at[9])
+    store_out = pltpu.make_async_copy(new_out_s, new_out, local_sem.at[10])
+
+    barrier = pltpu.get_barrier_semaphore()
+    each(
+        lambda p: pl.semaphore_signal(
+            barrier, inc=1, device_id={"dev": p}, device_id_type=MESH
+        )
+    )
+    own_tok.start()
+
+    def start_weights(c, carry):
+        gate_copy(c).start()
+        up_copy(c).start()
+        return carry
+
+    lax.fori_loop(0, CHUNKS, start_weights, 0)
+    pl.semaphore_wait(barrier, n - 1)
+    each(lambda p: send_tok(p).start())
+    each(lambda p: send_gout(p).start())
+    each(lambda p: send_gin(p).start())
+    own_gin.start()
+    own_gout.start()
+
+    def start_down(s, carry):
+        down_copy(lax.rem(s + 1, n)).start()
+        return carry
+
+    lax.fori_loop(0, n, start_down, 0)
+    for load in loads:
+        load.start()
+
+    accg[...] = jnp.zeros_like(accg)
+    accu[...] = jnp.zeros_like(accu)
+    own_tok.wait()
+    arrived(tok_s, tok_send, tok_recv)
+
+    packed = n * tok_s.shape[1]
+    shift = lax.broadcasted_iota(jnp.int32, (row_count, packed), 1) - (
+        CHUNKS * lax.broadcasted_iota(jnp.int32, (row_count, packed), 0)
+    )
+
+    def pick(c):
+        return jnp.where(shift == c, 1.0, 0.0).astype(jnp.bfloat16)
+
+    def project(c, carry):
+        tokens = tok_s[:, :, :width].reshape(packed, width)
+        block = jnp.dot(pick(c), tokens, preferred_element_type=jnp.float32).astype(
+            jnp.bfloat16
+        )
+        gate_copy(c).wait()
+        accg[...] += jnp.dot(block, gate_s[c], preferred_element_type=jnp.float32)
+        up_copy(c).wait()
+        accu[...] += jnp.dot(block, up_s[c], preferred_element_type=jnp.float32)
+        return carry
+
+    lax.fori_loop(0, CHUNKS, project, 0)
+    hot = jnp.dot(
+        pick(0),
+        tok_s[:, :, width:].reshape(packed, 128),
+        preferred_element_type=jnp.float32,
+    ).astype(jnp.bfloat16)
+    spread = jnp.where(
+        lax.broadcasted_iota(jnp.int32, (128, lanes), 1) // rank
+        == lax.broadcasted_iota(jnp.int32, (128, lanes), 0),
+        1.0,
+        0.0,
+    ).astype(jnp.bfloat16)
+    mask = jnp.dot(hot, spread, preferred_element_type=jnp.float32)
+    gated = accg[...]
+    hidden = (gated / (1.0 + jnp.exp(-gated)) * accu[...]).astype(jnp.bfloat16)
+
+    def project_down(s, carry):
+        p = other(s)
+        down_copy(s).wait()
+        part[p] = jnp.dot(hidden, down_s[s], preferred_element_type=jnp.float32).astype(
+            jnp.bfloat16
+        )
+        send_part(p).start()
+        return carry
+
+    lax.fori_loop(1, n, project_down, 0)
+    down_copy(0).wait()
+    own[...] = jnp.dot(hidden, down_s[0], preferred_element_type=jnp.float32)
+
+    def update(got, state, new_s, serve):
+        def block(i, carry):
+            rows = pl.ds(pl.multiple_of(lax.rem(i, rank // 16) * 16, 16), 16)
+            cols = pl.ds(pl.multiple_of(lax.div(i, rank // 16) * 128, 128), 128)
+            grads = [got[k, rows, cols].astype(jnp.float32) for k in range(n)]
+            for a in range(adapters):
+                total = owners[a * n : a * n + 1, :] * grads[0]
+                for k in range(1, n):
+                    total += owners[a * n + k : a * n + k + 1, :] * grads[k]
+                first = first_decay * state[1, a, rows, cols] + (1.0 - first_decay) * total
+                second = (
+                    second_decay * state[2, a, rows, cols]
+                    + (1.0 - second_decay) * total * total
+                )
+                value = state[0, a, rows, cols] - (learn_rate / first_fix) * first / (
+                    jnp.sqrt(second * (1.0 / second_fix)) + adam_eps
+                )
+                new_s[a, rows, cols] = value
+                at = pl.ds(pl.multiple_of(a * rank + lax.rem(i, rank // 16) * 16, 16), 16)
+                serve[at, cols] = value.astype(jnp.bfloat16)
+            return carry
+
+        lax.fori_loop(0, (rank // 16) * (got.shape[2] // 128), block, 0)
+
+    for load in loads:
+        load.wait()
+    own_gout.wait()
+    arrived(gout_s, gout_send, gout_recv)
+    update(gout_s, ad_out, new_out_s, serve_out)
+    store_out.start()
+    own_gin.wait()
+    arrived(gin_s, gin_send, gin_recv)
+    update(gin_s, ad_in, new_in_s, serve_in)
+    store_in.start()
+
+    every = lax.dot_general(
+        hidden, serve_in[...], (((1,), (1,)), ((), ())), preferred_element_type=jnp.float32
+    )
+    every = every * mask
+    inner = every[:, :128]
+    for q in range(1, lanes // 128):
+        inner += every[:, 128 * q : 128 * q + 128]
+    turn = 128
+    while turn > rank:
+        turn //= 2
+        inner += pltpu.roll(inner, turn, 1)
+    group = lax.broadcasted_iota(jnp.int32, (8, 128), 1) // rank
+    folded = jnp.zeros((8, 128), jnp.float32)
+    for q in range(row_count // 8):
+        folded += jnp.where(group == q, inner[8 * q : 8 * q + 8, :], 0.0)
+    got_inner[me] = folded
+    each(lambda p: send_inner(p).start())
+
+    arrived(got_part, part_send, part_recv)
+
+    def add_part(s, carry):
+        own[...] += got_part[other(s)].astype(jnp.float32)
+        return carry
+
+    lax.fori_loop(1, n, add_part, 0)
+
+    arrived(got_inner, inner_send, inner_recv)
+    inner_sum = got_inner[0]
+    for k in range(1, n):
+        inner_sum += got_inner[k]
+    inner_sum = inner_sum * (1.0 / math.sqrt(FFW))
+    pieces = []
+    for q in range(row_count // 8):
+        piece = jnp.where(group == q, inner_sum, 0.0)
+        turn = 128
+        while turn > rank:
+            turn //= 2
+            piece += pltpu.roll(piece, turn, 1)
+        pieces.append(piece)
+    lifted = jnp.concatenate(pieces, axis=0)
+    lifted = jnp.concatenate([lifted] * (lanes // 128), axis=1)
+    lifted = (lifted * mask).astype(jnp.bfloat16)
+    delta = jnp.dot(lifted, serve_out[...], preferred_element_type=jnp.float32)
+    result = own[...] + delta * (1.0 / math.sqrt(rank))
+    per = row_count // n
+    for j in range(n):
+        rows_out[j] = result[per * j : per * j + per, :]
+    each(lambda p: send_rows(p).start())
+    got_rows[me] = rows_out[me]
+    each(lambda p: send_tok(p).wait_send())
+    each(lambda p: send_gin(p).wait_send())
+    each(lambda p: send_gout(p).wait_send())
+    each(lambda p: send_part(p).wait_send())
+    each(lambda p: send_inner(p).wait_send())
+    store_in.wait()
+    store_out.wait()
+    arrived(got_rows, rows_send, rows_recv)
+    for j in range(n):
+        layer[:, column_block * j : column_block * (j + 1)] = got_rows[j].astype(jnp.bfloat16)
+    each(lambda p: send_rows(p).wait_send())
+
+
+def fused_shards(
+    tokens,
+    gate_weight,
+    up_weight,
+    down_weight,
+    grad_in,
+    grad_out,
+    adapter_in,
+    adapter_out,
+    moment_in,
+    moment_out,
+    second_in,
+    second_out,
+    tenants,
+    placement,
+    row_slot,
+):
+    n = lax.axis_size("dev")
+    me = lax.axis_index("dev")
+    per, model = tokens.shape
+    adapters, hidden_block, rank = adapter_in.shape
+    column_block = adapter_out.shape[2]
+    slots = placement.shape[1]
+    rows = n * per
+    width = model // CHUNKS
+    lanes = adapters * rank
+    code = jnp.arange(adapters, dtype=jnp.int32)
+    owners = (tenants[None, :] == code[:, None]).astype(jnp.float32).reshape(adapters * n, 1)
+    owners = jnp.broadcast_to(owners, (adapters * n, 128))
+    mine = (jnp.arange(n, dtype=jnp.int32) == me)[None, :, None, None]
+    slot = (row_slot[:, None] == jnp.arange(slots, dtype=jnp.int32)[None, :])[:, None, :, None]
+    held = placement[None, :, :, None] == jnp.arange(128, dtype=jnp.int32)[None, None, None, :]
+    hot = jnp.any(mine & slot & held, axis=(1, 2)).astype(jnp.bfloat16)
+    hot = jnp.broadcast_to(hot[:, None, :], (per, CHUNKS, 128)).reshape(per * CHUNKS, 128)
+    payload = jnp.concatenate([tokens.reshape(per * CHUNKS, width), hot], axis=1)
+    dma = pltpu.SemaphoreType.DMA
+    bf16, f32 = jnp.bfloat16, jnp.float32
+    vmem, hbm = pl.BlockSpec(memory_space=pltpu.VMEM), pl.BlockSpec(memory_space=pl.ANY)
+    layer, new_in, new_out = pl.pallas_call(
+        functools.partial(fused_kernel, n),
+        out_shape=(
+            jax.ShapeDtypeStruct((per, model), bf16),
+            jax.ShapeDtypeStruct((adapters, rank, hidden_block), f32),
+            jax.ShapeDtypeStruct((adapters, rank, column_block), f32),
+        ),
+        in_specs=[hbm] * 12 + [vmem],
+        out_specs=(vmem, hbm, hbm),
+        scratch_shapes=[
+            pltpu.VMEM((CHUNKS, width, hidden_block), bf16),
+            pltpu.VMEM((CHUNKS, width, hidden_block), bf16),
+            pltpu.VMEM((n, hidden_block, column_block), bf16),
+            pltpu.VMEM((n, per * CHUNKS, width + 128), bf16),
+            pltpu.VMEM((n, rank, hidden_block), bf16),
+            pltpu.VMEM((n, rank, column_block), bf16),
+            pltpu.VMEM((3, adapters, rank, hidden_block), f32),
+            pltpu.VMEM((3, adapters, rank, column_block), f32),
+            pltpu.VMEM((adapters, rank, hidden_block), f32),
+            pltpu.VMEM((adapters, rank, column_block), f32),
+            pltpu.VMEM((lanes, hidden_block), bf16),
+            pltpu.VMEM((lanes, column_block), bf16),
+            pltpu.VMEM((rows, hidden_block), f32),
+            pltpu.VMEM((rows, hidden_block), f32),
+            pltpu.VMEM((n, rows, column_block), bf16),
+            pltpu.VMEM((rows, column_block), f32),
+            pltpu.VMEM((n, rows, column_block), bf16),
+            pltpu.VMEM((n, 8, 128), f32),
+            pltpu.VMEM((n, per, column_block), f32),
+            pltpu.VMEM((n, per, column_block), f32),
+            dma((2 * CHUNKS + n,)),
+            dma((11,)),
+        ]
+        + [dma((n,))] * 12,
+        compiler_params=pltpu.CompilerParams(
+            collective_id=0, has_side_effects=True, vmem_limit_bytes=60 * 1024 * 1024
+        ),
+    )(
+        payload,
+        gate_weight,
+        up_weight,
+        down_weight,
+        jnp.swapaxes(grad_in[0], 0, 1),
+        grad_out[0],
+        jnp.swapaxes(adapter_in, 1, 2),
+        jnp.swapaxes(moment_in, 1, 2),
+        jnp.swapaxes(second_in, 1, 2),
+        adapter_out,
+        moment_out,
+        second_out,
+        owners,
+    )
+    return layer, jnp.swapaxes(new_in, 1, 2), new_out
+
+
+def fits(mesh, tokens, adapter_in, adapter_out):
+    n = mesh.shape["dev"]
+    per = tokens.shape[0] // (n * mesh.shape["groups"])
+    adapters = adapter_in.shape[0] // mesh.shape["groups"]
+    rank = adapter_in.shape[2]
+    return (
+        (adapter_in.shape[1] // n) % 128 == 0
+        and (adapter_out.shape[2] // n) % 128 == 0
+        and per * CHUNKS == 16
+        and tokens.shape[1] % (CHUNKS * 128) == 0
+        and 128 % rank == 0
+        and rank % 16 == 0
+        and adapters <= 128
+        and (adapters * rank) % 128 == 0
+        and n * per == 8 * (128 // rank)
+    )
+
+
 def solution(mesh):
     in_specs = (
         P(("groups", "dev"), None),
@@ -116,4 +559,11 @@
         P(("groups", "dev")),
     )
     out_specs = (P(("groups", "dev"), None), P("groups", "dev", None), P("groups", None, "dev"))
-    return jax.shard_map(shards, mesh=mesh, in_specs=in_specs, out_specs=out_specs, check_vma=False)
+
+    def program(*args):
+        body = fused_shards if fits(mesh, args[0], args[6], args[7]) else shards
+        return jax.shard_map(
+            body, mesh=mesh, in_specs=in_specs, out_specs=out_specs, check_vma=False
+        )(*args)
+
+    return program

time: 251 us -> 84 us (0.33)
  blocking collectives: 137 us -> 0 us
  Pallas kernels: 0 us -> 73 us
  local copies, waits for them, and re-layouts: 44.5 us -> 7.01 us
  matrix products: 26.9 us -> 0 us
  starting transfers between devices: 19 us -> 0 us
  between operations: 15 us -> 0.67 us
  other arithmetic: 7.96 us -> 2.96 us
    pallas_call x0 -> x1, Pallas kernels: none -> 73 us  [fused_shards(): pl.pallas_call(functools.partial(fused_kernel, n), out_shape=(jax.ShapeDt...]
    unnamed x1 -> x0, blocking collectives: 71.6 us -> none
    all_gather x2 -> x0, blocking collectives: 65.4 us -> none  [the longest x1 33.3 us: shards(): lax.all_gather(tokens, 'dev', axis=0, tiled=True)]
    dot_general x7 -> x0, matrix products: 26.9 us -> none  [the longest x1 7.66 us: shards(): upward = jnp.dot(all_tokens, up_weight, preferred_element_type=jnp.float32)]
    all_to_all x3 -> x0, starting transfers between devices: 18.8 us -> none  [the longest x1 7.39 us: shards(): lax.all_to_all(flat_out, 'dev', split_axis=1, concat_axis=1, tiled=True)]
    unnamed x34 -> x3, local copies, waits for them, and re-layouts: 19.5 us -> 5.43 us
    dot_general x2 -> x0, local copies, waits for them, and re-layouts: 9.67 us -> none  [shards(): jnp.einsum('an,nk->ak', owners, got_in[0], preferred_element_type=jnp.flo...]
    unnamed x3 -> x0, other arithmetic: 6.31 us -> none
  transfers between devices with their start and end apart: 4 -> 0, of which waited for: 0 -> 0; matrix products, arithmetic and copies ran while one was open for 30% -> 0% of each run, Pallas kernels for 0% -> 0%
where the time goes in v1:
time: 84 us; the launch traced here: 83.6 us
  Pallas kernels  73 us (87%)
  local copies, waits for them, and re-layouts  7.01 us (8%)
  other arithmetic  2.96 us (4%)
    pallas_call x1, Pallas kernels, fused_shards(): pl.pallas_call(functools.partial(fused_kernel, n), out_shape=(jax.ShapeDt...  73 us
    unnamed x3, local copies, waits for them, and re-layouts  5.43 us

profile of v1, /device:TPU:0, one launch (start us, length us, event | category | flops | bytes accessed | tf_op | source)
XLA Modules:
  0.0 83.6 jit_solution(14115626287948742614)
XLA Ops:
  0.6 0.7 iota_compare_fusion.2
  1.4 0.1 broadcast_and_fusion
  1.5 0.7 fusion
  2.1 0.1 reshape.74
  2.2 0.8 iota_compare_fusion
  3.0 0.1 and_reduce_fusion
  3.1 0.8 reshape.72
  3.9 0.6 pad_maximum_fusion.payload
  4.5 0.7 broadcast_in_dim.5.owners
  5.2 73.0 %shard_map.166 = (bf16[2,8192]{1,0:T(2,128)(2,1)}, f32[8,32,896]{2,1,0:T(8,128)}, f32[8,32,512]{2,1,0:T(8,128)}) custom-call(bf16[16,1152]{1,0:T(8,128)(2,1)} %pad_maximum_fusion.payload, bf16[8192,896]{1,0:T(8,128)(2,1)} %gate.1, bf16[8192,896]{1,0:T(8,128)(2,1)} %up.1, bf16[896,8192]{1,0:T(8,128)(2,1)} %down.1, bf16[32,14336]{1,0:T(8,128)(2,1)} %bitcast.11, ...), custom_call_target="tpu_custom_call" | custom-call | tf_op jit(solution)/shard_map/pallas_call | solution.py:470
  78.2 1.4 %copy.22 = bf16[2,8192]{1,0:T(2,128)(2,1)} copy(bf16[2,8192]{1,0:T(2,128)(2,1)} %get-tuple-element.12) | data formatting | bytes 65536
  79.6 2.2 %copy.23 = f32[8,896,32]{1,2,0:T(8,128)} copy(f32[8,896,32]{1,2,0:T(8,128)} %bitcast.10) | data formatting | bytes 1835008
  81.7 1.9 %copy.24 = f32[8,32,512]{2,1,0:T(8,128)} copy(f32[8,32,512]{2,1,0:T(8,128)} %get-tuple-element.14) | data formatting | bytes 1048576
  (3 shorter events, 0.0 us)

commit v2 on v1

--- a/solution.py
+++ b/solution.py
@@ -106,7 +106,10 @@
 
 def fused_kernel(
     n,
-    payload,
+    tokens,
+    tenants,
+    placement,
+    row_slot,
     gate,
     up,
     down,
@@ -118,7 +121,6 @@
     adapter_out,
     moment_out,
     second_out,
-    owners,
     layer,
     new_in,
     new_out,
@@ -136,9 +138,13 @@
     serve_out,
     accg,
     accu,
+    mate_part,
+    got_mate,
     part,
     own,
     got_part,
+    owners,
+    payload,
     got_inner,
     rows_out,
     got_rows,
@@ -150,6 +156,9 @@
     gin_recv,
     gout_send,
     gout_recv,
+    relay_send,
+    mate_send,
+    mate_recv,
     part_send,
     part_recv,
     inner_send,
@@ -161,12 +170,22 @@
     adapters, rank, hidden_block = ad_in.shape[1:]
     column_block = ad_out.shape[3]
     lanes = adapters * rank
-    width = payload.shape[1] - 128
+    width = tok_s.shape[2] - 128
     depth = gate_s.shape[1]
     row_count = accg.shape[0]
 
+    core = lax.rem(me, 2)
+    mate = me + 1 - 2 * core
+    half = n // 2
+
     def other(s):
         return lax.rem(me + s, n)
+
+    def chip(s):
+        return lax.rem(me + 2 * s, n)
+
+    def across(s):
+        return lax.rem(mate + 2 * s, n)
 
     def remote(src, dst, send, recv, peer):
         return pltpu.make_async_remote_copy(
@@ -185,6 +204,13 @@
 
         lax.fori_loop(1, n, step, 0)
 
+    def each_chip(body):
+        def step(s, carry):
+            body(chip(s))
+            return carry
+
+        lax.fori_loop(1, half, step, 0)
+
     def hid(j):
         return pl.ds(pl.multiple_of(j * hidden_block, 128), hidden_block)
 
@@ -192,7 +218,18 @@
         return pl.ds(pl.multiple_of(j * column_block, 128), column_block)
 
     def send_tok(p):
-        return remote(payload, tok_s.at[me], tok_send.at[p], tok_recv.at[me], p)
+        return remote(tok_s.at[me], tok_s.at[me], tok_send.at[p], tok_recv.at[me], p)
+
+    def relay(p):
+        return remote(tok_s.at[p], tok_s.at[p], relay_send.at[p], tok_recv.at[p], mate)
+
+    def tok_arrived(p):
+        return remote(tok_s.at[p], tok_s.at[p], tok_send.at[p], tok_recv.at[p], p)
+
+    def send_mate(s):
+        return remote(
+            mate_part.at[s], got_mate.at[s], mate_send.at[s], mate_recv.at[s], mate
+        )
 
     def send_gin(p):
         return remote(
@@ -226,12 +263,11 @@
         rows = pl.ds(pl.multiple_of(c * depth, 128), depth)
         return pltpu.make_async_copy(up.at[rows, :], up_s.at[c], weight_sem.at[CHUNKS + c])
 
-    def down_copy(s):
+    def down_copy(s, p):
         return pltpu.make_async_copy(
-            down.at[:, col(other(s))], down_s.at[s], weight_sem.at[2 * CHUNKS + s]
-        )
-
-    own_tok = pltpu.make_async_copy(payload, tok_s.at[me], local_sem.at[0])
+            down.at[:, col(p)], down_s.at[s], weight_sem.at[2 * CHUNKS + s]
+        )
+
     own_gin = pltpu.make_async_copy(grad_in.at[:, hid(me)], gin_s.at[me], local_sem.at[1])
     own_gout = pltpu.make_async_copy(grad_out.at[:, col(me)], gout_s.at[me], local_sem.at[2])
     loads = [
@@ -256,7 +292,6 @@
             barrier, inc=1, device_id={"dev": p}, device_id_type=MESH
         )
     )
-    own_tok.start()
 
     def start_weights(c, carry):
         gate_copy(c).start()
@@ -264,25 +299,55 @@
         return carry
 
     lax.fori_loop(0, CHUNKS, start_weights, 0)
+    values = tokens[...].astype(jnp.float32)
+    lane = lax.broadcasted_iota(jnp.int32, (CHUNKS, 128), 1)
+    for r in range(row_count // n):
+        for c in range(CHUNKS):
+            payload[r * CHUNKS + c : r * CHUNKS + c + 1, :width] = values[
+                r : r + 1, c * width : (c + 1) * width
+            ]
+        chosen = placement[row_slot[r], me]
+        payload[r * CHUNKS : (r + 1) * CHUNKS, width:] = jnp.where(lane == chosen, 1.0, 0.0)
+    tok_s[me] = payload[...].astype(jnp.bfloat16)
     pl.semaphore_wait(barrier, n - 1)
-    each(lambda p: send_tok(p).start())
+    send_tok(mate).start()
+    each_chip(lambda p: send_tok(p).start())
+    each(lambda p: send_gin(p).start())
     each(lambda p: send_gout(p).start())
-    each(lambda p: send_gin(p).start())
     own_gin.start()
     own_gout.start()
 
-    def start_down(s, carry):
-        down_copy(lax.rem(s + 1, n)).start()
-        return carry
-
-    lax.fori_loop(0, n, start_down, 0)
+    def start_across(s, carry):
+        down_copy(s, across(s)).start()
+        return carry
+
+    def start_chip(s, carry):
+        down_copy(half + s, chip(s)).start()
+        return carry
+
+    lax.fori_loop(0, half, start_across, 0)
+    lax.fori_loop(0, half, start_chip, 0)
     for load in loads:
         load.start()
 
     accg[...] = jnp.zeros_like(accg)
     accu[...] = jnp.zeros_like(accu)
-    own_tok.wait()
-    arrived(tok_s, tok_send, tok_recv)
+    code = lax.broadcasted_iota(jnp.int32, (adapters, 128), 0)
+    for k in range(n):
+        owners[k * adapters : (k + 1) * adapters, :] = jnp.where(code == tenants[k], 1.0, 0.0)
+
+    def pass_on(p):
+        tok_arrived(p).wait_recv()
+        relay(p).start()
+
+    each_chip(pass_on)
+    tok_arrived(mate).wait_recv()
+
+    def relayed(s, carry):
+        tok_arrived(across(s)).wait_recv()
+        return carry
+
+    lax.fori_loop(1, half, relayed, 0)
 
     packed = n * tok_s.shape[1]
     shift = lax.broadcasted_iota(jnp.int32, (row_count, packed), 1) - (
@@ -319,18 +384,29 @@
     gated = accg[...]
     hidden = (gated / (1.0 + jnp.exp(-gated)) * accu[...]).astype(jnp.bfloat16)
 
-    def project_down(s, carry):
-        p = other(s)
-        down_copy(s).wait()
-        part[p] = jnp.dot(hidden, down_s[s], preferred_element_type=jnp.float32).astype(
-            jnp.bfloat16
-        )
+    def down_across(s, carry):
+        down_copy(s, across(s)).wait()
+        mate_part[s] = jnp.dot(hidden, down_s[s], preferred_element_type=jnp.float32)
+        send_mate(s).start()
+        return carry
+
+    lax.fori_loop(0, half, down_across, 0)
+
+    def down_chip(s, carry):
+        p = chip(s)
+        down_copy(half + s, p).wait()
+        whole = jnp.dot(hidden, down_s[half + s], preferred_element_type=jnp.float32)
+        send_mate(s).wait_recv()
+        part[p] = (whole + got_mate[s]).astype(jnp.bfloat16)
         send_part(p).start()
         return carry
 
-    lax.fori_loop(1, n, project_down, 0)
-    down_copy(0).wait()
-    own[...] = jnp.dot(hidden, down_s[0], preferred_element_type=jnp.float32)
+    lax.fori_loop(1, half, down_chip, 0)
+    down_copy(half, me).wait()
+    send_mate(0).wait_recv()
+    own[...] = got_mate[0] + jnp.dot(
+        hidden, down_s[half], preferred_element_type=jnp.float32
+    )
 
     def update(got, state, new_s, serve):
         def block(i, carry):
@@ -338,9 +414,9 @@
             cols = pl.ds(pl.multiple_of(lax.div(i, rank // 16) * 128, 128), 128)
             grads = [got[k, rows, cols].astype(jnp.float32) for k in range(n)]
             for a in range(adapters):
-                total = owners[a * n : a * n + 1, :] * grads[0]
+                total = owners[a : a + 1, :] * grads[0]
                 for k in range(1, n):
-                    total += owners[a * n + k : a * n + k + 1, :] * grads[k]
+                    total += owners[k * adapters + a : k * adapters + a + 1, :] * grads[k]
                 first = first_decay * state[1, a, rows, cols] + (1.0 - first_decay) * total
                 second = (
                     second_decay * state[2, a, rows, cols]
@@ -358,10 +434,6 @@
 
     for load in loads:
         load.wait()
-    own_gout.wait()
-    arrived(gout_s, gout_send, gout_recv)
-    update(gout_s, ad_out, new_out_s, serve_out)
-    store_out.start()
     own_gin.wait()
     arrived(gin_s, gin_send, gin_recv)
     update(gin_s, ad_in, new_in_s, serve_in)
@@ -385,13 +457,17 @@
     got_inner[me] = folded
     each(lambda p: send_inner(p).start())
 
-    arrived(got_part, part_send, part_recv)
-
-    def add_part(s, carry):
-        own[...] += got_part[other(s)].astype(jnp.float32)
-        return carry
-
-    lax.fori_loop(1, n, add_part, 0)
+    own_gout.wait()
+    arrived(gout_s, gout_send, gout_recv)
+    update(gout_s, ad_out, new_out_s, serve_out)
+    store_out.start()
+
+    def add_part(p):
+        send = remote(got_part.at[p], got_part.at[p], part_send.at[p], part_recv.at[p], p)
+        send.wait_recv()
+        own[...] += got_part[p].astype(jnp.float32)
+
+    each_chip(add_part)
 
     arrived(got_inner, inner_send, inner_recv)
     inner_sum = got_inner[0]
@@ -416,10 +492,18 @@
         rows_out[j] = result[per * j : per * j + per, :]
     each(lambda p: send_rows(p).start())
     got_rows[me] = rows_out[me]
-    each(lambda p: send_tok(p).wait_send())
+    send_tok(mate).wait_send()
+    each_chip(lambda p: send_tok(p).wait_send())
+    each_chip(lambda p: relay(p).wait_send())
     each(lambda p: send_gin(p).wait_send())
     each(lambda p: send_gout(p).wait_send())
-    each(lambda p: send_part(p).wait_send())
+    each_chip(lambda p: send_part(p).wait_send())
+
+    def mate_sent(s, carry):
+        send_mate(s).wait_send()
+        return carry
+
+    lax.fori_loop(0, half, mate_sent, 0)
     each(lambda p: send_inner(p).wait_send())
     store_in.wait()
     store_out.wait()
@@ -427,6 +511,30 @@
     for j in range(n):
         layer[:, column_block * j : column_block * (j + 1)] = got_rows[j].astype(jnp.bfloat16)
     each(lambda p: send_rows(p).wait_send())
+
+
+def copy_kernel(*refs):
+    sources, targets, sems = refs[:3], refs[3:6], refs[6]
+    copies = [
+        pltpu.make_async_copy(source, target, sems.at[i])
+        for i, (source, target) in enumerate(zip(sources, targets))
+    ]
+    for copy in copies:
+        copy.start()
+    for copy in copies:
+        copy.wait()
+
+
+def hand_over(*arrays):
+    hbm = pl.BlockSpec(memory_space=pl.ANY)
+    return pl.pallas_call(
+        copy_kernel,
+        out_shape=tuple(jax.ShapeDtypeStruct(a.shape, a.dtype) for a in arrays),
+        in_specs=[pl.BlockSpec(memory_space=pltpu.VMEM)] * 3,
+        out_specs=(hbm,) * 3,
+        scratch_shapes=[pltpu.SemaphoreType.DMA((3,))],
+        compiler_params=pltpu.CompilerParams(vmem_limit_bytes=60 * 1024 * 1024),
+    )(*arrays)
 
 
 def fused_shards(
@@ -447,26 +555,16 @@
     row_slot,
 ):
     n = lax.axis_size("dev")
-    me = lax.axis_index("dev")
     per, model = tokens.shape
     adapters, hidden_block, rank = adapter_in.shape
     column_block = adapter_out.shape[2]
-    slots = placement.shape[1]
     rows = n * per
     width = model // CHUNKS
     lanes = adapters * rank
-    code = jnp.arange(adapters, dtype=jnp.int32)
-    owners = (tenants[None, :] == code[:, None]).astype(jnp.float32).reshape(adapters * n, 1)
-    owners = jnp.broadcast_to(owners, (adapters * n, 128))
-    mine = (jnp.arange(n, dtype=jnp.int32) == me)[None, :, None, None]
-    slot = (row_slot[:, None] == jnp.arange(slots, dtype=jnp.int32)[None, :])[:, None, :, None]
-    held = placement[None, :, :, None] == jnp.arange(128, dtype=jnp.int32)[None, None, None, :]
-    hot = jnp.any(mine & slot & held, axis=(1, 2)).astype(jnp.bfloat16)
-    hot = jnp.broadcast_to(hot[:, None, :], (per, CHUNKS, 128)).reshape(per * CHUNKS, 128)
-    payload = jnp.concatenate([tokens.reshape(per * CHUNKS, width), hot], axis=1)
     dma = pltpu.SemaphoreType.DMA
     bf16, f32 = jnp.bfloat16, jnp.float32
     vmem, hbm = pl.BlockSpec(memory_space=pltpu.VMEM), pl.BlockSpec(memory_space=pl.ANY)
+    smem = pl.BlockSpec(memory_space=pltpu.SMEM)
     layer, new_in, new_out = pl.pallas_call(
         functools.partial(fused_kernel, n),
         out_shape=(
@@ -474,7 +572,7 @@
             jax.ShapeDtypeStruct((adapters, rank, hidden_block), f32),
             jax.ShapeDtypeStruct((adapters, rank, column_block), f32),
         ),
-        in_specs=[hbm] * 12 + [vmem],
+        in_specs=[vmem] + [smem] * 3 + [hbm] * 11,
         out_specs=(vmem, hbm, hbm),
         scratch_shapes=[
             pltpu.VMEM((CHUNKS, width, hidden_block), bf16),
@@ -491,21 +589,28 @@
             pltpu.VMEM((lanes, column_block), bf16),
             pltpu.VMEM((rows, hidden_block), f32),
             pltpu.VMEM((rows, hidden_block), f32),
+            pltpu.VMEM((n // 2, rows, column_block), f32),
+            pltpu.VMEM((n // 2, rows, column_block), f32),
             pltpu.VMEM((n, rows, column_block), bf16),
             pltpu.VMEM((rows, column_block), f32),
             pltpu.VMEM((n, rows, column_block), bf16),
+            pltpu.VMEM((n * adapters, 128), f32),
+            pltpu.VMEM((per * CHUNKS, width + 128), f32),
             pltpu.VMEM((n, 8, 128), f32),
             pltpu.VMEM((n, per, column_block), f32),
             pltpu.VMEM((n, per, column_block), f32),
             dma((2 * CHUNKS + n,)),
             dma((11,)),
         ]
-        + [dma((n,))] * 12,
+        + [dma((n,))] * 15,
         compiler_params=pltpu.CompilerParams(
             collective_id=0, has_side_effects=True, vmem_limit_bytes=60 * 1024 * 1024
         ),
     )(
-        payload,
+        tokens,
+        tenants,
+        jnp.swapaxes(placement, 0, 1),
+        row_slot,
         gate_weight,
         up_weight,
         down_weight,
@@ -517,8 +622,8 @@
         adapter_out,
         moment_out,
         second_out,
-        owners,
-    )
+    )
+    layer, new_in, new_out = hand_over(layer, new_in, new_out)
     return layer, jnp.swapaxes(new_in, 1, 2), new_out
 
 
@@ -528,7 +633,8 @@
     adapters = adapter_in.shape[0] // mesh.shape["groups"]
     rank = adapter_in.shape[2]
     return (
-        (adapter_in.shape[1] // n) % 128 == 0
+        n % 2 == 0
+        and (adapter_in.shape[1] // n) % 128 == 0
         and (adapter_out.shape[2] // n) % 128 == 0
         and per * CHUNKS == 16
         and tokens.shape[1] % (CHUNKS * 128) == 0

time: 84 us -> 64.6 us (0.77)
  Pallas kernels: 73 us -> 63.8 us
  local copies, waits for them, and re-layouts: 7.01 us -> 0 us
  other arithmetic: 2.96 us -> 0 us
    pallas_call x1, Pallas kernels: 73 us -> 61.3 us  [fused_shards(): pl.pallas_call(functools.partial(fused_kernel, n), out_shape=(jax.ShapeDt...]
    unnamed x3 -> x0, local copies, waits for them, and re-layouts: 5.43 us -> none
    pallas_call x0 -> x1, Pallas kernels: none -> 2.47 us  [hand_over(): pl.pallas_call(copy_kernel, out_shape=tuple((jax.ShapeDtypeStruct(a.shape...]
    eq x3 -> x0, other arithmetic: 1.49 us -> none  [the longest x1 0.76 us: fused_shards(): placement[None, :, :, None]]
where the time goes in v2:
time: 64.6 us; the launch traced here: 64.4 us
  Pallas kernels  63.8 us (99%)
    pallas_call x1, Pallas kernels, fused_shards(): pl.pallas_call(functools.partial(fused_kernel, n), out_shape=(jax.ShapeDt...  61.3 us
    pallas_call x1, Pallas kernels, hand_over(): pl.pallas_call(copy_kernel, out_shape=tuple((jax.ShapeDtypeStruct(a.shape...  2.47 us

profile of v2, /device:TPU:0, one launch (start us, length us, event | category | flops | bytes accessed | tf_op | source)
XLA Modules:
  0.0 64.4 jit_solution(12694941686839192046)
XLA Ops:
  0.6 61.3 %shard_map.166 = (bf16[2,8192]{1,0:T(2,128)(2,1)}, f32[8,32,896]{2,1,0:T(8,128)}, f32[8,32,512]{2,1,0:T(8,128)}) custom-call(bf16[2,8192]{1,0:T(2,128)(2,1)} %tokens.1, s32[16]{0:T(128)} %tenants.1, s32[4,16]{1,0:T(4,128)} %bitcast.14, s32[2]{0:T(128)} %row_slot.1, bf16[8192,896]{1,0:T(8,128)(2,1)} %gate.1, bf16[8192,896]{1,0:T(8,128)(2,1)} %up.1, ...), custom_call_target="tpu_custom_call" | custom-call | tf_op jit(solution)/shard_map/pallas_call | solution.py:568
  61.9 2.5 %shard_map.167 = (bf16[2,8192]{1,0:T(2,128)(2,1)}, f32[8,32,896]{2,1,0:T(8,128)}, f32[8,32,512]{2,1,0:T(8,128)}) custom-call(bf16[2,8192]{1,0:T(2,128)(2,1)} %get-tuple-element.9.refs_0_, f32[8,32,896]{2,1,0:T(8,128)} %get-tuple-element.10.refs_1_, f32[8,32,512]{2,1,0:T(8,128)} %get-tuple-element.11.refs_2_), custom_call_target="tpu_custom_call" | custom-call | tf_op jit(solution)/shard_map/pallas_call | solution.py:530
